TPU v7x, 128 devices: a whole 4x4x4 slice. The times are simulated.
128 devices in a mesh: section: 8 (over z, x_hi), ctx: 8 (over y, core), head: 2 (over x_lo).
Axes of the slice: x: 4 (x_hi: 2, x_lo: 2; x = x_hi * 2 + x_lo), y: 4, z: 4, core: 2. Of those that a mesh axis runs over, the one named last changes fastest.
Arguments:
- queries: bfloat16 [8, 2560, 5120], P('section', 'ctx', 'head'), may hold values from -6 to 6
- out_grad: bfloat16 [8, 2560, 5120], P('section', 'ctx', 'head'), may hold values from -12 to 12
- keys: bfloat16 [2560, 1024], P(('section', 'ctx'), 'head'), may hold values from -6 to 6
- values: bfloat16 [2560, 1024], P(('section', 'ctx'), 'head'), may hold values from -6 to 6
Outputs:
- query_grad: bfloat16 [8, 2560, 5120], P('section', 'ctx', 'head')
- key_grad: bfloat16 [2560, 1024], P(('section', 'ctx'), 'head')
- value_grad: bfloat16 [2560, 1024], P(('section', 'ctx'), 'head')
All inputs are finite; a program needn't handle non-finite values.
Results may differ from a plain program's by a relative error of at most 0.0089.
Values may be sent and summed in bfloat16 or wider, within the bound.
A program may use at most 64 MiB of HBM per device.

v0:
```python
import jax
import jax.numpy as jnp
from jax import lax
from jax.sharding import PartitionSpec as P

HEAD_DIM = 128


def attend_rows(query_rows, grad_rows, first_row, key_all, value_all, key_acc, value_acc):
    row_count = query_rows.shape[0]
    kv_local = query_rows.shape[1]
    groups = query_rows.shape[2]
    key_width = min(256, key_all.shape[0])
    scale_factor = query_rows.shape[-1] ** (-0.5)
    positions = first_row + jnp.arange(row_count, dtype=jnp.int32)
    block_count = (first_row + row_count - 1) // key_width + 1

    def block_terms(block_index):
        key_start = block_index * key_width
        key_block = lax.dynamic_slice_in_dim(key_all, key_start, key_width, 0)
        value_block = lax.dynamic_slice_in_dim(value_all, key_start, key_width, 0)
        key_places = key_start + jnp.arange(key_width, dtype=jnp.int32)
        visible = key_places[None, :] <= positions[:, None]
        scores = (
            jnp.einsum("rhgd,khd->hgrk", query_rows, key_block, preferred_element_type=jnp.float32)
            * scale_factor
        )
        scores = jnp.where(visible[None, None], scores, -jnp.inf)
        out_dots = jnp.einsum(
            "rhgd,khd->hgrk", grad_rows, value_block, preferred_element_type=jnp.float32
        )
        return (key_start, key_block, scores, out_dots)

    def first_pass(block_index, state_now):
        row_max, row_sum, cross_sum = state_now
        key_start, key_block, scores, out_dots = block_terms(block_index)
        new_max = jnp.maximum(row_max, scores.max(-1))
        shrink = jnp.exp(row_max - new_max)
        weights = jnp.exp(scores - new_max[..., None])
        row_sum = row_sum * shrink + weights.sum(-1)
        cross_sum = cross_sum * shrink + (weights * out_dots).sum(-1)
        return (new_max, row_sum, cross_sum)

    stat_shape = (kv_local, groups, row_count)
    initial = (
        jnp.full(stat_shape, -jnp.inf, jnp.float32),
        jnp.zeros(stat_shape, jnp.float32),
        jnp.zeros(stat_shape, jnp.float32),
    )
    row_max, row_sum, cross_sum = lax.fori_loop(0, block_count, first_pass, initial)
    row_delta = cross_sum / row_sum

    def second_pass(block_index, state_now):
        query_sum, key_acc, value_acc = state_now
        key_start, key_block, scores, out_dots = block_terms(block_index)
        soft_probs = jnp.exp(scores - row_max[..., None]) / row_sum[..., None]
        probs_low = soft_probs.astype(jnp.bfloat16)
        score_grad = (soft_probs * (out_dots - row_delta[..., None])).astype(jnp.bfloat16)
        query_sum = query_sum + jnp.einsum(
            "hgrk,khd->rhgd", score_grad, key_block, preferred_element_type=jnp.float32
        )
        key_part = (
            jnp.einsum("hgrk,rhgd->khd", score_grad, query_rows, preferred_element_type=jnp.float32)
            * scale_factor
        )
        value_part = jnp.einsum(
            "hgrk,rhgd->khd", probs_low, grad_rows, preferred_element_type=jnp.float32
        )
        key_old = lax.dynamic_slice_in_dim(key_acc, key_start, key_width, 0)
        value_old = lax.dynamic_slice_in_dim(value_acc, key_start, key_width, 0)
        key_acc = lax.dynamic_update_slice_in_dim(key_acc, key_old + key_part, key_start, 0)
        value_acc = lax.dynamic_update_slice_in_dim(value_acc, value_old + value_part, key_start, 0)
        return (query_sum, key_acc, value_acc)

    query_sum = jnp.zeros(query_rows.shape, jnp.float32)
    query_sum, key_acc, value_acc = lax.fori_loop(
        0, block_count, second_pass, (query_sum, key_acc, value_acc)
    )
    return (query_sum * scale_factor, key_acc, value_acc)


def shards(queries, out_grad, keys, values):
    layers, row_count, columns = queries.shape
    kv_local = keys.shape[1] // HEAD_DIM
    groups = columns // keys.shape[1]
    key_all, value_all = (
        lax.all_gather(keys, ("section", "ctx"), axis=0, tiled=True),
        lax.all_gather(values, ("section", "ctx"), axis=0, tiled=True),
    )
    key_all = key_all.reshape(-1, kv_local, HEAD_DIM)
    value_all = value_all.reshape(-1, kv_local, HEAD_DIM)
    ctx_place = lax.axis_index("ctx")
    key_acc = jnp.zeros(key_all.shape, jnp.float32)
    value_acc = jnp.zeros(key_all.shape, jnp.float32)
    query_rows = queries[0].reshape(row_count, kv_local, groups, HEAD_DIM)
    grad_rows = out_grad[0].reshape(row_count, kv_local, groups, HEAD_DIM)
    query_part, key_acc, value_acc = attend_rows(
        query_rows, grad_rows, ctx_place * row_count, key_all, value_all, key_acc, value_acc
    )
    results = [query_part.reshape(row_count, columns).astype(jnp.bfloat16)]
    query_grad = jnp.stack(results)
    key_total, value_total = (
        lax.psum_scatter(key_acc, ("section", "ctx"), scatter_dimension=0, tiled=True),
        lax.psum_scatter(value_acc, ("section", "ctx"), scatter_dimension=0, tiled=True),
    )
    key_grad = key_total.reshape(key_total.shape[0], kv_local * HEAD_DIM).astype(jnp.bfloat16)
    value_grad = value_total.reshape(value_total.shape[0], kv_local * HEAD_DIM).astype(jnp.bfloat16)
    return (query_grad, key_grad, value_grad)


def solution(mesh):
    in_specs = (
        P("section", "ctx", "head"),
        P("section", "ctx", "head"),
        P(("section", "ctx"), "head"),
        P(("section", "ctx"), "head"),
    )
    out_specs = (
        P("section", "ctx", "head"),
        P(("section", "ctx"), "head"),
        P(("section", "ctx"), "head"),
    )
    return jax.shard_map(shards, mesh=mesh, in_specs=in_specs, out_specs=out_specs, check_vma=False)
```

profile of v0, /device:TPU:16, one launch (start us, length us, event | category | flops | bytes accessed | tf_op | source)
XLA Modules:
  0.0 1089.8 jit_solution(10798346780709517121)
XLA Ops:
  8.7 4.0 copy.27
  20.9 60.0 %all-gather.3.cloned.1.call-done = bf16[2560,512]{1,0:T(8,128)(2,1)} async-done(((bf16[40,512]{1,0:T(8,128)(2,1)}), bf16[2560,512]{1,0:T(8,128)(2,1)}) %all-gather.3.cloned.1.call-update) | async-done | bytes 2621456 | tf_op jit(solution)/shard_map/all_gather | solution.py:87
  81.0 4.4 copy.26
  85.3 4.4 copy.34
  89.8 60.7 %all-gather.5.cloned.1.call-done = bf16[2560,512]{1,0:T(8,128)(2,1)} async-done(((bf16[40,512]{1,0:T(8,128)(2,1)}), bf16[2560,512]{1,0:T(8,128)(2,1)}) %all-gather.5.cloned.1.call-update) | async-done | bytes 2621456 | tf_op jit(solution)/shard_map/all_gather | solution.py:88
  150.5 4.4 copy.28
  154.8 4.4 copy.32
  159.3 66.8 %while.30 = (s32[]{:T(128)}, f32[4,5,320]{2,1,0:T(8,128)S(1)}, f32[4,5,320]{2,1,0:T(8,128)S(1)}, f32[4,5,320]{2,1,0:T(8,128)S(1)}, s32[]{:T(128)}, /*index=5*/bf...) while((s32[]{:T(128)}, f32[4,5,320]{2,1,0:T(8,128)S(1)}, ...), condition=%wide.region_4.5_spmd.clone, body=%wide.region_0.4_spmd.clone.sunk | while | flops 858623296 | bytes 24255172 | solution.py:50
  161.9 4.1 fusion.75
  171.4 4.1 fusion.75
  180.9 4.1 fusion.75
  190.5 4.1 fusion.75
  200.0 4.1 fusion.75
  209.6 4.1 fusion.75
  219.1 4.1 fusion.75
  233.5 110.2 %while.31 = (s32[]{:T(128)}, f32[320,4,5,128]{3,0,2,1:T(8,128)}, f32[2560,4,128]{2,0,1:T(8,128)}, f32[2560,4,128]{2,0,1:T(8,128)}, s32[]{:T(128)}, /*index=5*/bf...) while((s32[]{:T(128)}, f32[320,4,5,128]{3,0,2,1:T(8,128)}, ...), condition=%wide.region_6.7_spmd.clone, body=%wide.region_5.6_spmd.clone.sunk | while | flops 2111554048 | bytes 71941920 | solution.py:76
  239.0 3.4 fusion.90
  245.7 3.6 fusion.89
  254.8 3.4 fusion.90
  261.4 3.6 fusion.89
  270.5 3.4 fusion.90
  277.2 3.6 fusion.89
  286.2 3.4 fusion.90
  292.9 3.6 fusion.89
  302.0 3.4 fusion.90
  308.7 3.6 fusion.89
  317.8 3.4 fusion.90
  324.4 3.6 fusion.89
  333.5 3.4 fusion.90
  340.2 3.6 fusion.89
  353.3 391.4 %reduce-scatter.5.cloned.1.call-done = f32[40,4,128]{2,0,1:T(8,128)} async-done(((f32[2560,4,128]{2,0,1:T(8,128)}), f32[40,4,128]{2,0,1:T(8,128)}) %reduce-scatter.5.cloned.1.call-update) | async-done | bytes 81936 | tf_op jit(solution)/shard_map/reduce_scatter | solution.py:104
  746.2 335.5 %reduce-scatter.3.cloned.1.call-done = f32[40,4,128]{2,0,1:T(8,128)} async-done(((f32[2560,4,128]{2,0,1:T(8,128)}), f32[40,4,128]{2,0,1:T(8,128)}) %reduce-scatter.3.cloned.1.call-update) | async-done | bytes 81936 | tf_op jit(solution)/shard_map/reduce_scatter | solution.py:103
  (153 shorter events, 128.2 us)
Async XLA Ops:
  7.2 73.8 %all-gather.3.cloned.1.call-start = ((), (), s32[]{:S(2)}) async-start(), calls=%async_computation.2 | async-start | bytes 2662400 | tf_op jit(solution)/shard_map/all_gather | solution.py:87
  7.9 142.6 %all-gather.5.cloned.1.call-start = ((), (), s32[]{:S(2)}) async-start(), calls=%async_computation.3 | async-start | bytes 2662400 | tf_op jit(solution)/shard_map/all_gather | solution.py:88
  8.6 736.1 %reduce-scatter.5.cloned.1.call-start = ((), (), s32[]{:S(2)}) async-start(), calls=%async_computation.5 | async-start | bytes 5324800 | tf_op jit(solution)/shard_map/reduce_scatter | solution.py:104
  8.7 6.9 copy-start.3
  239.0 3.4 copy-start
  245.7 3.6 copy-start.1
  254.8 3.4 copy-start
  261.4 3.6 copy-start.1
  270.5 3.4 copy-start
  277.2 3.6 copy-start.1
  286.2 3.4 copy-start
  292.9 3.6 copy-start.1
  302.0 3.4 copy-start
  308.7 3.6 copy-start.1
  317.7 3.4 copy-start
  324.4 3.6 copy-start.1
  333.5 3.4 copy-start
  340.1 3.6 copy-start.1
  343.8 1.9 copy-start.2
  343.8 737.9 %reduce-scatter.3.cloned.1.call-start = ((), (), s32[]{:S(2)}) async-start(), calls=%async_computation.4 | async-start | bytes 5324800 | tf_op jit(solution)/shard_map/reduce_scatter | solution.py:103
Sparse Core Ops, SparseCore 0:
  11.3 69.5 all-gather.2
  84.3 66.1 all-gather.4
  343.9 400.7 reduce-scatter.4
  747.0 334.7 reduce-scatter.2
where the time goes:
time: 1110 us; the launch traced here: 1090 us
  waiting for transfers between devices  850 us (77%)
  matrix products  155 us (14%)
  local copies, waits for them, and re-layouts  44.7 us (4%)
  other arithmetic  25.9 us (2%)
  between operations  13.9 us (1%)
    reduce_scatter x1, waiting for transfers between devices, shards(): lax.psum_scatter(value_acc, ('section', 'ctx'), scatter_dimension=0, tile...  391 us
    reduce_scatter x1, waiting for transfers between devices, shards(): lax.psum_scatter(key_acc, ('section', 'ctx'), scatter_dimension=0, tiled=...  336 us
    all_gather x1, waiting for transfers between devices, shards(): lax.all_gather(values, ('section', 'ctx'), axis=0, tiled=True)  60.7 us
    all_gather x1, waiting for transfers between devices, shards(): lax.all_gather(keys, ('section', 'ctx'), axis=0, tiled=True)  60 us
    dot_general x14, matrix products, block_terms(): jnp.einsum('rhgd,khd->hgrk', grad_rows, value_block, preferred_element_ty...  46 us
    dot_general x14, matrix products, block_terms(): jnp.einsum('rhgd,khd->hgrk', query_rows, key_block, preferred_element_typ...  36.9 us
    unnamed x11, local copies, waits for them, and re-layouts  25.6 us
    dot_general x7, matrix products, second_pass(): jnp.einsum('hgrk,rhgd->khd', score_grad, query_rows, preferred_element_ty...  25.2 us
  transfers between devices with their start and end apart: 4, of which 4 were waited for; matrix products, arithmetic and copies ran while one was open for 3% of the time, Pallas kernels for 0%

commit v1 on v0

v1 whole, which is shorter than its diff:
```python
import functools

import jax
import jax.numpy as jnp
from jax import lax
from jax.experimental import pallas as pl
from jax.experimental.pallas import tpu as pltpu
from jax.sharding import PartitionSpec as P

HD = 128
LOG2E = 1.4426950408889634
bf16, f32 = jnp.bfloat16, jnp.float32
MESH = pl.DeviceIdType.MESH
Z, X, Y, C = 4, 2, 4, 2


def dot_nt(a, b):
    return lax.dot_general(a, b, (((1,), (1,)), ((), ())), preferred_element_type=f32)


def dot_tn(a, b):
    return lax.dot_general(a, b, (((0,), (0,)), ((), ())), preferred_element_type=f32)


def in_pairs(count, step):
    @pl.loop(0, count // 2)
    def _(i):
        step(2 * i)
        step(2 * i + 1)

    @pl.loop(count // 2 * 2, count)
    def _(i):
        step(i)


STREAMS = ((0, 0, 48, "yz"), (0, 48, 32, "zy"), (1, 0, 80, "zy"), (2, 0, 80, "yz"), (3, 0, 80, "zy"))


def kernel(q_hbm, do_hbm, k_in, v_in, dq_hbm, dk_out, dv_out,
           kv, qf, dof, qs, k2, vv, s_ref, d_ref, m_ref, l_ref, c_ref, dqt, dq_st,
           dk_acc, dv_acc, own, keep_z, keep_y, cs, cr, zs, zr, ys, yr, xs, xr,
           in_sem, dq_sem, gx, gs, gc, rc, rz, ry, rx):
    rows = q_hbm.shape[0]
    share = k_in.shape[0]
    heads = k_in.shape[1] // HD
    groups = q_hbm.shape[1] // k_in.shape[1]
    flat = rows * groups
    scale = HD ** -0.5
    section, ctx, half = lax.axis_index("section"), lax.axis_index("ctx"), lax.axis_index("head")
    z, x, y, c = section // X, section % X, ctx // C, ctx % C
    place = ctx
    blocks = place + 1

    def device(z, x, y, c):
        return (z * X + x, y * C + c, half)

    y_at = [device(z, x, (y + d) % Y, c) for d in range(1, Y)]
    z_at = [device((z + d) % Z, x, y, c) for d in range(1, Z)]
    x_at = device(z, 1 - x, y, c)
    c_at = device(z, x, y, 1 - c)

    def load(h, g, which):
        source, target = ((q_hbm, qf), (do_hbm, dof))[which]
        cols = pl.ds(pl.multiple_of((h * groups + g) * HD, HD), HD)
        return pltpu.make_async_copy(
            source.at[:, cols], target.at[h, pl.ds(g * rows, rows), :], in_sem.at[which, h, g])

    for h in range(heads):
        for g in range(groups):
            load(h, g, 0).start()
            load(h, g, 1).start()

    barrier = pltpu.get_barrier_semaphore()
    partners = y_at + z_at + [x_at, c_at]
    for partner in partners:
        pl.semaphore_signal(barrier, inc=1, device_id=partner, device_id_type=MESH)
    for h in range(heads):
        cols = slice(h * HD, (h + 1) * HD)
        pair = jnp.concatenate([k_in[:, cols].astype(f32), v_in[:, cols].astype(f32)], axis=0)
        kv[h, z, x, y, c] = pair.astype(bf16)
    pl.semaphore_wait(barrier, len(partners))

    def copy(src, dst, sems, index, where):
        return pltpu.make_async_remote_copy(
            src_ref=src, dst_ref=dst, send_sem=sems.at[(0,) + index], recv_sem=sems.at[(1,) + index],
            device_id=where, device_id_type=MESH)

    near = {"y": y_at, "z": z_at}

    def gather_x():
        part = kv.at[:, z, x, y, c]
        return copy(part, part, gx, (), x_at)

    def gather_step(n, step, d):
        h, first, count, order = STREAMS[n]
        some = pl.ds(first, count)
        if step == 0:
            part = kv.at[h, z, :, y, c, some]
        elif order[0] == "y":
            part = kv.at[h, z, :, :, c, some]
        else:
            part = kv.at[h, :, :, y, c, some]
        return copy(part, part, gs, (n, step, d - 1), near[order[step]][d - 1])

    def gather_c(h):
        part = kv.at[h, :, :, :, c]
        return copy(part, part, gc, (h,), c_at)

    def streams_of(h):
        return [n for n in range(len(STREAMS)) if STREAMS[n][0] == h]

    def start_step(h, step):
        for n in streams_of(h):
            for d in range(1, 4):
                gather_step(n, step, d).start()

    def end_step(h, step):
        for n in streams_of(h):
            for d in range(1, 4):
                gather_step(n, step, d).wait_recv()

    gather_x().start()
    gather_x().wait_recv()
    for h in range(heads):
        start_step(h, 0)
    end_step(0, 0)
    start_step(0, 1)
    end_step(0, 1)
    gather_c(0).start()
    for h in range(1, heads):
        end_step(h, 0)
        start_step(h, 1)

    def sum_c(h):
        return copy(cs, cr.at[h % 2], rc, (h,), c_at)

    def sum_z(h, d):
        return copy(zs.at[d - 1], zr.at[h % 2, d - 1], rz, (h, d - 1), z_at[d - 1])

    def sum_y(h, d):
        return copy(ys.at[d - 1], yr.at[h, d - 1], ry, (h, d - 1), y_at[d - 1])

    def sum_x(h):
        return copy(xs, xr.at[h], rx, (h,), x_at)

    def sum_first(h):
        @pl.when(h >= 1)
        def _():
            sum_c(h - 1).wait_send()

        for i in range(Z * X):
            for core, put in ((1 - c, True), (c, False)):
                pair = jnp.concatenate([dk_acc[i, :, core], dv_acc[i, :, core]], axis=1)
                if put:
                    cs[i // X, i % X] = pair.astype(bf16)
                else:
                    own[i // X, i % X] = pair
        sum_c(h).start()

    def sum_second(h):
        sum_c(h).wait_recv()

        @pl.when(h >= 1)
        def _():
            for d in range(1, Z):
                sum_z(h - 1, d).wait_send()

        for d in range(1, Z):
            i = (z + d) % Z
            zs[d - 1] = (own[i] + cr[h % 2, i].astype(f32)).astype(bf16)
            sum_z(h, d).start()
        keep_z[h % 2] = own[z] + cr[h % 2, z].astype(f32)

    def sum_third(h):
        for d in range(1, Z):
            sum_z(h, d).wait_recv()
        total = keep_z[h % 2]
        for d in range(1, Z):
            total = total + zr[h % 2, d - 1].astype(f32)
        keep_z[h % 2] = total

        @pl.when(h >= 1)
        def _():
            for d in range(1, Y):
                sum_y(h - 1, d).wait_send()

        for d in range(1, Y):
            ys[d - 1] = keep_z[h % 2, :, (y + d) % Y].astype(bf16)
            sum_y(h, d).start()

    def sum_fourth(h):
        for d in range(1, Y):
            sum_y(h, d).wait_recv()
        total = keep_z[h % 2, :, y]
        for d in range(1, Y):
            total = total + yr[h, d - 1].astype(f32)
        keep_y[...] = total

        @pl.when(h >= 1)
        def _():
            sum_x(h - 1).wait_send()

        xs[...] = keep_y[1 - x].astype(bf16)
        sum_x(h).start()

    def sum_last(h):
        sum_x(h).wait_recv()
        total = keep_y[x] + xr[h].astype(f32)
        cols = pl.ds(pl.multiple_of(h * HD, HD), HD)
        dk_out[:, cols] = (total[:share] * scale).astype(bf16)
        dv_out[:, cols] = total[share:].astype(bf16)

    def write_dq(h, g):
        cols = pl.ds(pl.multiple_of((h * groups + g) * HD, HD), HD)
        return pltpu.make_async_copy(
            dq_st.at[h % 2, pl.ds(g * rows, rows), :], dq_hbm.at[:, cols], dq_sem.at[h % 2, g])

    row_id = lax.rem(lax.broadcasted_iota(jnp.int32, (1, flat), 1), rows)
    key_id = lax.broadcasted_iota(jnp.int32, (rows, flat), 0)

    def head(h, carry):
        for g in range(groups):
            load(h, g, 0).wait()
            load(h, g, 1).wait()
        gather_c(h).wait_recv()
        wide = qf[h].astype(f32) * (scale * LOG2E)
        high = wide.astype(bf16)
        qs[:, :HD] = high
        qs[:, HD:] = (wide - high.astype(f32)).astype(bf16)

        @pl.loop(0, Z * X)
        def _(i):
            at = pl.ds(pl.multiple_of(i * rows, rows), rows)
            pair = kv[h, i // X, i % X].astype(f32)
            key = pair[:, :, :share].reshape(rows, HD).astype(bf16)
            k2[at, :HD] = key
            k2[at, HD:] = key
            vv[at, :] = pair[:, :, share:].reshape(rows, HD).astype(bf16)

        @pl.when(h >= 2)
        def _():
            sum_third(h - 2)

        @pl.when(h >= 3)
        def _():
            sum_last(h - 3)

        m_ref[...] = jnp.full_like(m_ref, -1e30)
        l_ref[...] = jnp.zeros_like(l_ref)
        c_ref[...] = jnp.zeros_like(c_ref)
        dqt[...] = jnp.zeros_like(dqt)

        def front(b, masked):
            at = pl.ds(pl.multiple_of(b * rows, rows), rows)
            s = dot_nt(k2[at, :], qs[...])
            if masked:
                s = jnp.where(key_id <= row_id, s, -jnp.inf)
            d = dot_nt(vv[at, :], dof[h])
            s_ref[at, :] = s
            d_ref[at, :] = d
            s = s_ref[at, :].reshape(rows // 8, 8, flat)
            d = d_ref[at, :].reshape(rows // 8, 8, flat)
            old = m_ref[...]
            new = jnp.maximum(old, s.max(0))
            fade = jnp.exp2(old - new)
            e = jnp.exp2(s - new)
            l_ref[...] = l_ref[...] * fade + e.sum(0)
            c_ref[...] = c_ref[...] * fade + (e * d).sum(0)
            m_ref[...] = new

        in_pairs(place, lambda b: front(b, False))
        front(place, True)

        for following in range(1, heads):
            @pl.when(h == following - 1)
            def _():
                end_step(following, 1)
                gather_c(following).start()

        @pl.when(h >= 1)
        def _():
            sum_second(h - 1)

        @pl.when(h >= 2)
        def _():
            sum_fourth(h - 2)

        top8 = m_ref[...]
        top = top8.max(0, keepdims=True)
        fade = jnp.exp2(top8 - top)
        total = (l_ref[...] * fade).sum(0, keepdims=True)
        lse = jnp.broadcast_to(top + jnp.log2(total), (8, flat))
        delta = jnp.broadcast_to((c_ref[...] * fade).sum(0, keepdims=True) / total, (8, flat))

        def back(b):
            at = pl.ds(pl.multiple_of(b * rows, rows), rows)
            p = jnp.exp2(s_ref[at, :].reshape(rows // 8, 8, flat) - lse)
            ds = p * (d_ref[at, :].reshape(rows // 8, 8, flat) - delta)
            p = p.reshape(rows, flat).astype(bf16)
            ds = ds.reshape(rows, flat).astype(bf16)
            dv_acc[b] = jnp.dot(p, dof[h], preferred_element_type=f32).reshape(Y, C, share, HD)
            dk_acc[b] = jnp.dot(ds, qf[h], preferred_element_type=f32).reshape(Y, C, share, HD)
            dqt[...] += dot_tn(k2[at, :HD], ds)

        in_pairs(blocks, back)

        @pl.loop(blocks, Z * X)
        def _(b):
            dv_acc[b] = jnp.zeros((Y, C, share, HD), f32)
            dk_acc[b] = jnp.zeros((Y, C, share, HD), f32)

        @pl.when(h >= 2)
        def _():
            for g in range(groups):
                write_dq(h - 2, g).wait()

        dq_st[h % 2] = (dqt[...] * scale).T.astype(bf16)
        for g in range(groups):
            write_dq(h, g).start()
        sum_first(h)
        return carry

    lax.fori_loop(0, heads, head, 0)

    last = heads - 1
    sum_third(last - 1)
    sum_second(last)
    sum_last(last - 2)
    sum_fourth(last - 1)
    sum_third(last)
    sum_last(last - 1)
    sum_fourth(last)
    sum_last(last)
    gather_x().wait_send()
    for h in range(heads):
        gather_c(h).wait_send()
        for n in streams_of(h):
            for d in range(1, 4):
                gather_step(n, 0, d).wait_send()
                gather_step(n, 1, d).wait_send()
    sum_c(last).wait_send()
    sum_x(last).wait_send()
    for d in range(1, 4):
        sum_z(last, d).wait_send()
        sum_y(last, d).wait_send()
    for h in (last - 1, last):
        for g in range(groups):
            write_dq(h, g).wait()


def shards(queries, out_grad, keys, values):
    _, rows, cols = queries.shape
    share, key_cols = keys.shape
    heads = key_cols // HD
    groups = cols // key_cols
    flat = rows * groups
    seq = rows * Z * X
    pair = (2 * share, HD)
    V = pltpu.VMEM
    sem = pltpu.SemaphoreType.DMA
    any_space = pl.BlockSpec(memory_space=pl.ANY)
    in_vmem = pl.BlockSpec(memory_space=pltpu.VMEM)
    dq, dk, dv = pl.pallas_call(
        kernel,
        in_specs=[any_space, any_space, in_vmem, in_vmem],
        out_specs=[any_space, in_vmem, in_vmem],
        out_shape=[jax.ShapeDtypeStruct((rows, cols), bf16),
                   jax.ShapeDtypeStruct((share, key_cols), bf16),
                   jax.ShapeDtypeStruct((share, key_cols), bf16)],
        scratch_shapes=[
            V((heads, Z, X, Y, C) + pair, bf16),
            V((heads, flat, HD), bf16), V((heads, flat, HD), bf16),
            V((flat, 2 * HD), bf16), V((seq, 2 * HD), bf16), V((seq, HD), bf16),
            V((seq, flat), f32), V((seq, flat), f32),
            V((8, flat), f32), V((8, flat), f32), V((8, flat), f32),
            V((HD, flat), f32), V((2, flat, HD), bf16),
            V((Z * X, Y, C, share, HD), f32), V((Z * X, Y, C, share, HD), f32),
            V((Z, X, Y) + pair, f32), V((2, X, Y) + pair, f32), V((X,) + pair, f32),
            V((Z, X, Y) + pair, bf16), V((2, Z, X, Y) + pair, bf16),
            V((Z - 1, X, Y) + pair, bf16), V((2, Z - 1, X, Y) + pair, bf16),
            V((Y - 1, X) + pair, bf16), V((heads, Y - 1, X) + pair, bf16),
            V(pair, bf16), V((heads,) + pair, bf16),
            sem((2, heads, groups)), sem((2, groups)),
            sem((2,)), sem((2, len(STREAMS), 2, 3)), sem((2, heads)),
            sem((2, heads)), sem((2, heads, Z - 1)), sem((2, heads, Y - 1)), sem((2, heads)),
        ],
        compiler_params=pltpu.CompilerParams(
            collective_id=0, has_side_effects=True, vmem_limit_bytes=65400 << 10),
    )(queries[0], out_grad[0], keys, values)
    return dq[None], dk, dv


def solution(mesh):
    wide = P("section", "ctx", "head")
    tall = P(("section", "ctx"), "head")
    return jax.shard_map(shards, mesh=mesh, in_specs=(wide, wide, tall, tall),
                         out_specs=(wide, tall, tall), check_vma=False)
```

time: 1110 us -> 110 us (0.10); the launches traced: 1090 us -> 108 us
  waiting for transfers between devices: 850 us -> 0 us
  matrix products: 155 us -> 0 us
  Pallas kernels: 0 us -> 104 us
  local copies, waits for them, and re-layouts: 44.7 us -> 3.96 us
  other arithmetic: 25.9 us -> 0 us
  between operations: 13.9 us -> 0.66 us
    reduce_scatter x2 -> x0, waiting for transfers between devices: 727 us -> none  [the longest x1 391 us: shards(): lax.psum_scatter(value_acc, ('section', 'ctx'), scatter_dimension=0, tile...]
    dot_general x49 -> x0, matrix products: 155 us -> none  [the longest x14 46 us: block_terms(): jnp.einsum('rhgd,khd->hgrk', grad_rows, value_block, preferred_element_ty...]
    all_gather x2 -> x0, waiting for transfers between devices: 121 us -> none  [the longest x1 60.7 us: shards(): lax.all_gather(values, ('section', 'ctx'), axis=0, tiled=True)]
    pallas_call x0 -> x1, Pallas kernels: none -> 104 us  [shards(): pl.pallas_call(kernel, in_specs=[any_space, any_space, in_vmem, in_vmem],...]
    unnamed x11 -> x7, local copies, waits for them, and re-layouts: 25.6 us -> 3.96 us
    reduce_sum x7 -> x0, other arithmetic: 19.2 us -> none  [first_pass(): row_sum = row_sum * shrink + weights.sum(-1)]
  transfers between devices with their start and end apart: 4 -> 0, of which waited for: 4 -> 0; matrix products, arithmetic and copies ran while one was open for 3% -> 0% of each run, Pallas kernels for 0% -> 0%
where the time goes in v1:
time: 110 us; the launch traced here: 108 us
  Pallas kernels  104 us (95%)
  local copies, waits for them, and re-layouts  3.96 us (4%)
    pallas_call x1, Pallas kernels, shards(): pl.pallas_call(kernel, in_specs=[any_space, any_space, in_vmem, in_vmem],...  104 us
    unnamed x7, local copies, waits for them, and re-layouts  3.96 us

profile of v1, /device:TPU:16, one launch (start us, length us, event | category | flops | bytes accessed | tf_op | source)
XLA Modules:
  0.0 108.2 jit_solution(15076170907393313446)
XLA Ops:
  0.6 103.6 %shard_map.67 = (bf16[320,2560]{1,0:T(8,128)(2,1)}, bf16[40,512]{1,0:T(8,128)(2,1)}, bf16[40,512]{1,0:T(8,128)(2,1)}) custom-call(bf16[320,2560]{1,0:T(8,128)(2,1)} %bitcast.3, bf16[320,2560]{1,0:T(8,128)(2,1)} %bitcast.4, bf16[40,512]{1,0:T(8,128)(2,1)} %k_in.1, bf16[40,512]{1,0:T(8,128)(2,1)} %v_in.1), custom_call_target="tpu_custom_call" | custom-call | tf_op jit(solution)/shard_map/pallas_call | solution.py:363
  104.3 0.0 copy-start.1
  104.3 0.0 copy-start
  104.3 2.7 %copy.10 = bf16[1,320,2560]{2,1,0:T(8,128)(2,1)} copy(bf16[1,320,2560]{2,1,0:T(8,128)(2,1)} %bitcast.5) | data formatting | bytes 3276800
  107.0 0.0 copy-done.1
  107.0 0.6 copy.11
  107.6 0.0 copy-done
  107.6 0.6 copy.12
Async XLA Ops:
  104.3 2.7 %copy-start.1 = (bf16[40,512]{1,0:T(8,128)(2,1)S(1)}, bf16[40,512]{1,0:T(8,128)(2,1)}, u32[]{:S(2)}) copy-start(bf16[40,512]{1,0:T(8,128)(2,1)} %get-tuple-element.13) | copy-start | bytes 122884
  104.3 3.4 %copy-start = (bf16[40,512]{1,0:T(8,128)(2,1)S(1)}, bf16[40,512]{1,0:T(8,128)(2,1)}, u32[]{:S(2)}) copy-start(bf16[40,512]{1,0:T(8,128)(2,1)} %get-tuple-element.14) | copy-start | bytes 122884

commit v2 on v1

v2 whole, which is shorter than its diff:
```python
import functools

import jax
import jax.numpy as jnp
from jax import lax
from jax.experimental import pallas as pl
from jax.experimental.pallas import tpu as pltpu
from jax.sharding import PartitionSpec as P

HD = 128
LOG2E = 1.4426950408889634
bf16, f32 = jnp.bfloat16, jnp.float32
MESH = pl.DeviceIdType.MESH
Z, X, Y, C = 4, 2, 4, 2


def dot_nt(a, b):
    return lax.dot_general(a, b, (((1,), (1,)), ((), ())), preferred_element_type=f32)


def dot_tn(a, b):
    return lax.dot_general(a, b, (((0,), (0,)), ((), ())), preferred_element_type=f32)


def in_pairs(count, step):
    @pl.loop(0, count // 2)
    def _(i):
        step(2 * i)
        step(2 * i + 1)

    @pl.loop(count // 2 * 2, count)
    def _(i):
        step(i)


CTX = Y * C
SHIP = ((0, 4, 0), (5, 5, 1), (6, 7, 2))


def kernel(q_hbm, do_hbm, k_in, v_in, dq_hbm, dk_out, dv_out,
           kv, qf, dof, fq, fdo, qs, k2, vv, s_ref, d_ref, m_ref, l_ref, c_ref, dqt, dq_st, fdq_st,
           dk_acc, dv_acc, own_sum, keep_b, keep_y, cs, cr, bs, br, ys, yr,
           in_sem, dq_sem, ship_sem, back_sem, gy, gb, gc, rc, rb, ry):
    rows = q_hbm.shape[0]
    share = k_in.shape[0]
    heads = k_in.shape[1] // HD
    groups = q_hbm.shape[1] // k_in.shape[1]
    flat = rows * groups
    scale = HD ** -0.5
    section, ctx, half = lax.axis_index("section"), lax.axis_index("ctx"), lax.axis_index("head")
    z, x, y, c = section // X, section % X, ctx // C, ctx % C

    def device(z, x, y, c):
        return (z * X + x, y * C + c, half)

    y_at = [device(z, x, (y + d) % Y, c) for d in range(1, Y)]
    c_at = device(z, x, y, 1 - c)
    others = [(dz, dx) for dz in range(Z) for dx in range(X) if dz or dx]
    block_of = [((z + dz) % Z, (x + dx) % X) for dz, dx in others]
    block_at = [device(bz, bx, y, c) for bz, bx in block_of]

    def load(h, g, which):
        source, target = ((q_hbm, qf), (do_hbm, dof))[which]
        cols = pl.ds(pl.multiple_of((h * groups + g) * HD, HD), HD)
        return pltpu.make_async_copy(
            source.at[:, cols], target.at[h, pl.ds(g * rows, rows), :], in_sem.at[which, h, g])

    mirror = (section, CTX - 1 - ctx, half)

    def shipped(h, i, count, which):
        source, target = ((q_hbm, fq), (do_hbm, fdo))[which]
        cols = pl.ds(pl.multiple_of(((h + 1) * groups - count + i) * HD, HD), HD)
        return pltpu.make_async_remote_copy(
            src_ref=source.at[:, cols], dst_ref=target.at[h, pl.ds(i * rows, rows), :],
            send_sem=ship_sem.at[0, which, h, i], recv_sem=ship_sem.at[1, which, h, i],
            device_id=mirror, device_id_type=MESH)

    def returned(h, i, count):
        cols = pl.ds(pl.multiple_of(((h + 1) * groups - count + i) * HD, HD), HD)
        return pltpu.make_async_remote_copy(
            src_ref=fdq_st.at[h % 2, pl.ds(i * rows, rows), :], dst_ref=dq_hbm.at[:, cols],
            send_sem=back_sem.at[0, h, i], recv_sem=back_sem.at[1, h, i],
            device_id=mirror, device_id_type=MESH)

    owners = [(low <= ctx, ctx <= high, count) for low, high, count in SHIP]
    owners = [(jnp.logical_and(over, under), count) for over, under, count in owners]
    helpers = [(low <= CTX - 1 - ctx, CTX - 1 - ctx <= high, count) for low, high, count in SHIP]
    helpers = [(jnp.logical_and(over, under), count) for over, under, count in helpers if count]

    for is_owner, count in owners:
        @pl.when(is_owner)
        def _():
            for h in range(heads):
                for g in range(groups - count):
                    load(h, g, 0).start()
                    load(h, g, 1).start()

    barrier = pltpu.get_barrier_semaphore()
    partners = y_at + block_at + [c_at, mirror]
    for partner in partners:
        pl.semaphore_signal(barrier, inc=1, device_id=partner, device_id_type=MESH)
    for h in range(heads):
        cols = slice(h * HD, (h + 1) * HD)
        pair = jnp.concatenate([k_in[:, cols].astype(f32), v_in[:, cols].astype(f32)], axis=0)
        kv[h, z, x, y, c] = pair.astype(bf16)
    pl.semaphore_wait(barrier, len(partners))

    def copy(src, dst, sems, index, where):
        return pltpu.make_async_remote_copy(
            src_ref=src, dst_ref=dst, send_sem=sems.at[(0,) + index], recv_sem=sems.at[(1,) + index],
            device_id=where, device_id_type=MESH)

    def gather_y(d):
        part = kv.at[:, z, x, y, c]
        return copy(part, part, gy, (d - 1,), y_at[d - 1])

    def gather_b(h, i):
        part = kv.at[h, z, x, :, c]
        return copy(part, part, gb, (h, i), block_at[i])

    def gather_c(h):
        part = kv.at[h, :, :, :, c]
        return copy(part, part, gc, (h,), c_at)

    def start_blocks(h):
        for i in range(len(others)):
            gather_b(h, i).start()

    def end_blocks(h):
        for i in range(len(others)):
            gather_b(h, i).wait_recv()

    def ship(heads_now):
        for is_owner, count in owners:
            if count:
                @pl.when(is_owner)
                def _():
                    for h in heads_now:
                        for i in range(count):
                            shipped(h, i, count, 0).start()
                            shipped(h, i, count, 1).start()

    for d in range(1, Y):
        gather_y(d).start()
    ship([0])
    for d in range(1, Y):
        gather_y(d).wait_recv()
    start_blocks(0)
    ship(range(1, heads))
    end_blocks(0)
    gather_c(0).start()
    start_blocks(1)
    start_blocks(2)

    def sum_c(h):
        return copy(cs, cr.at[h % 2], rc, (h,), c_at)

    def sum_b(h, i):
        return copy(bs.at[i], br.at[h, i], rb, (h, i), block_at[i])

    def sum_y(h, d):
        return copy(ys.at[d - 1], yr.at[h, d - 1], ry, (h, d - 1), y_at[d - 1])

    def sum_first(h):
        @pl.when(h >= 1)
        def _():
            sum_c(h - 1).wait_send()

        for i in range(Z * X):
            for core, put in ((1 - c, True), (c, False)):
                pair = jnp.concatenate([dk_acc[i, :, core], dv_acc[i, :, core]], axis=1)
                if put:
                    cs[i // X, i % X] = pair.astype(bf16)
                else:
                    own_sum[i // X, i % X] = pair
        sum_c(h).start()

    def sum_second(h):
        sum_c(h).wait_recv()

        @pl.when(h >= 1)
        def _():
            for i in range(len(others)):
                sum_b(h - 1, i).wait_send()

        for i, (bz, bx) in enumerate(block_of):
            bs[i] = (own_sum[bz, bx] + cr[h % 2, bz, bx].astype(f32)).astype(bf16)
            sum_b(h, i).start()
        keep_b[h % 2] = own_sum[z, x] + cr[h % 2, z, x].astype(f32)

    def sum_third(h):
        total = keep_b[h % 2]
        for i in range(len(others)):
            sum_b(h, i).wait_recv()
            total = total + br[h, i].astype(f32)

        @pl.when(h >= 1)
        def _():
            for d in range(1, Y):
                sum_y(h - 1, d).wait_send()

        keep_y[...] = total
        for d in range(1, Y):
            ys[d - 1] = keep_y[(y + d) % Y].astype(bf16)
            sum_y(h, d).start()

    def sum_last(h):
        total = keep_y[y]
        for d in range(1, Y):
            sum_y(h, d).wait_recv()
            total = total + yr[h, d - 1].astype(f32)
        cols = pl.ds(pl.multiple_of(h * HD, HD), HD)
        dk_out[:, cols] = (total[:share] * scale).astype(bf16)
        dv_out[:, cols] = total[share:].astype(bf16)

    def write_dq(h, g):
        cols = pl.ds(pl.multiple_of((h * groups + g) * HD, HD), HD)
        return pltpu.make_async_copy(
            dq_st.at[h % 2, pl.ds(g * rows, rows), :], dq_hbm.at[:, cols], dq_sem.at[h % 2, g])

    def lanes_of(width):
        return [(j, min(HD, width - j)) for j in range(0, width, HD)]

    def begin(width, place, q_part, do_part):
        lanes = lanes_of(width)
        wide = q_part[...].astype(f32) * (scale * LOG2E)
        high = wide.astype(bf16)
        qs[:width, :HD] = high
        qs[:width, HD:] = (wide - high.astype(f32)).astype(bf16)
        m_ref[:, :width] = jnp.full((8, width), -1e30, f32)
        l_ref[:, :width] = jnp.zeros((8, width), f32)
        c_ref[:, :width] = jnp.zeros((8, width), f32)
        dqt[:, :width] = jnp.zeros((HD, width), f32)

        def front(b, masked):
            at = pl.ds(pl.multiple_of(b * rows, rows), rows)
            s = dot_nt(k2[at, :], qs[:width, :])
            if masked:
                row_id = lax.rem(lax.broadcasted_iota(jnp.int32, (1, width), 1), rows)
                key_id = lax.broadcasted_iota(jnp.int32, (rows, width), 0)
                s = jnp.where(key_id <= row_id, s, -jnp.inf)
            d = dot_nt(vv[at, :], do_part[...])
            for n, (j, w) in enumerate(lanes):
                s_ref[b * len(lanes) + n, :, :w] = s[:, j:j + w]
                d_ref[b * len(lanes) + n, :, :w] = d[:, j:j + w]
            for n, (j, w) in enumerate(lanes):
                s = s_ref[b * len(lanes) + n, :, :w].reshape(rows // 8, 8, w)
                d = d_ref[b * len(lanes) + n, :, :w].reshape(rows // 8, 8, w)
                some = slice(j, j + w)
                old = m_ref[:, some]
                new = jnp.maximum(old, s.max(0))
                fade = jnp.exp2(old - new)
                e = jnp.exp2(s - new)
                l_ref[:, some] = l_ref[:, some] * fade + e.sum(0)
                c_ref[:, some] = c_ref[:, some] * fade + (e * d).sum(0)
                m_ref[:, some] = new

        in_pairs(place, lambda b: front(b, False))
        front(place, True)
        top8 = m_ref[:, :width]
        top = top8.max(0, keepdims=True)
        fade = jnp.exp2(top8 - top)
        total = (l_ref[:, :width] * fade).sum(0, keepdims=True)
        m_ref[:, :width] = jnp.broadcast_to(top + jnp.log2(total), (8, width))
        l_ref[:, :width] = jnp.broadcast_to(
            (c_ref[:, :width] * fade).sum(0, keepdims=True) / total, (8, width))

    def finish(width, place, q_part, do_part, own_part):
        lanes = lanes_of(width)

        def back(b):
            at = pl.ds(pl.multiple_of(b * rows, rows), rows)
            ps, dss = [], []
            for n, (j, w) in enumerate(lanes):
                s = s_ref[b * len(lanes) + n, :, :w].reshape(rows // 8, 8, w)
                d = d_ref[b * len(lanes) + n, :, :w].reshape(rows // 8, 8, w)
                p = jnp.exp2(s - m_ref[:, j:j + w])
                ds = p * (d - l_ref[:, j:j + w])
                ps.append(p.reshape(rows, w).astype(bf16))
                dss.append(ds.reshape(rows, w).astype(bf16))
            p, ds = jnp.concatenate(ps, axis=1), jnp.concatenate(dss, axis=1)
            dv = jnp.dot(p, do_part[...], preferred_element_type=f32).reshape(Y, C, share, HD)
            dk = jnp.dot(ds, q_part[...], preferred_element_type=f32).reshape(Y, C, share, HD)
            if own_part:
                dv_acc[b] = dv
                dk_acc[b] = dk
            else:
                dv_acc[b] += dv
                dk_acc[b] += dk
            dqt[:, :width] += dot_tn(k2[at, :HD], ds)

        in_pairs(place + 1, back)

    def head(h, carry):
        gather_c(h).wait_recv()

        @pl.loop(0, Z * X)
        def _(i):
            at = pl.ds(pl.multiple_of(i * rows, rows), rows)
            pair = kv[h, i // X, i % X].astype(f32)
            key = pair[:, :, :share].reshape(rows, HD).astype(bf16)
            k2[at, :HD] = key
            k2[at, HD:] = key
            vv[at, :] = pair[:, :, share:].reshape(rows, HD).astype(bf16)

        @pl.when(h >= 3)
        def _():
            sum_last(h - 3)

        def own(count):
            width = (groups - count) * rows
            return width, ctx, qf.at[h, :width], dof.at[h, :width]

        def foreign(count):
            width = count * rows
            return width, CTX - 1 - ctx, fq.at[h, :width], fdo.at[h, :width]

        def own_end(count):
            width = (groups - count) * rows
            finish(*own(count), True)

            @pl.when(h >= 2)
            def _():
                for g in range(groups - count):
                    write_dq(h - 2, g).wait()

            dq_st[h % 2, :width] = (dqt[:, :width] * scale).T.astype(bf16)
            for g in range(groups - count):
                write_dq(h, g).start()

            @pl.loop(ctx + 1, Z * X)
            def _(b):
                dv_acc[b] = jnp.zeros((Y, C, share, HD), f32)
                dk_acc[b] = jnp.zeros((Y, C, share, HD), f32)

        def foreign_begin(count):
            for i in range(count):
                shipped(h, i, count, 0).wait_recv()
                shipped(h, i, count, 1).wait_recv()
            begin(*foreign(count))

        def foreign_end(count):
            width = count * rows
            finish(*foreign(count), False)

            @pl.when(h >= 2)
            def _():
                for i in range(count):
                    returned(h - 2, i, count).wait_send()

            fdq_st[h % 2, :width] = (dqt[:, :width] * scale).T.astype(bf16)
            for i in range(count):
                returned(h, i, count).start()

        for is_owner, count in owners:
            @pl.when(is_owner)
            def _():
                for g in range(groups - count):
                    load(h, g, 0).wait()
                    load(h, g, 1).wait()
                begin(*own(count))

        @pl.when(ctx <= 1)
        def _():
            own_end(0)
            foreign_begin(2)

        for following in range(1, heads):
            @pl.when(h == following - 1)
            def _():
                end_blocks(following)
                gather_c(following).start()
                if following == 1:
                    start_blocks(3)

        @pl.when(h >= 1)
        def _():
            sum_second(h - 1)

        @pl.when(h >= 2)
        def _():
            sum_third(h - 2)

        for is_owner, count in owners:
            @pl.when(jnp.logical_and(is_owner, ctx >= 2))
            def _():
                own_end(count)

        @pl.when(ctx <= 1)
        def _():
            foreign_end(2)

        @pl.when(ctx == 2)
        def _():
            foreign_begin(1)
            foreign_end(1)

        sum_first(h)
        return carry

    lax.fori_loop(0, heads, head, 0)

    last = heads - 1
    sum_second(last)
    sum_last(last - 2)
    sum_third(last - 1)
    sum_last(last - 1)
    sum_third(last)
    sum_last(last)
    for d in range(1, Y):
        gather_y(d).wait_send()
        sum_y(last, d).wait_send()
    for h in range(heads):
        gather_c(h).wait_send()
        for i in range(len(others)):
            gather_b(h, i).wait_send()
    sum_c(last).wait_send()
    for i in range(len(others)):
        sum_b(last, i).wait_send()
    for is_owner, count in owners:
        @pl.when(is_owner)
        def _():
            for h in range(heads):
                for i in range(count):
                    shipped(h, i, count, 0).wait_send()
                    shipped(h, i, count, 1).wait_send()
                    returned(h, i, count).wait_recv()
            for h in (last - 1, last):
                for g in range(groups - count):
                    write_dq(h, g).wait()
    for is_helper, count in helpers:
        @pl.when(is_helper)
        def _():
            for h in (last - 1, last):
                for i in range(count):
                    returned(h, i, count).wait_send()


def shards(queries, out_grad, keys, values):
    _, rows, cols = queries.shape
    share, key_cols = keys.shape
    heads = key_cols // HD
    groups = cols // key_cols
    flat = rows * groups
    seq = rows * Z * X
    pair = (2 * share, HD)
    V = pltpu.VMEM
    sem = pltpu.SemaphoreType.DMA
    any_space = pl.BlockSpec(memory_space=pl.ANY)
    in_vmem = pl.BlockSpec(memory_space=pltpu.VMEM)
    dq, dk, dv = pl.pallas_call(
        kernel,
        in_specs=[any_space, any_space, in_vmem, in_vmem],
        out_specs=[any_space, in_vmem, in_vmem],
        out_shape=[jax.ShapeDtypeStruct((rows, cols), bf16),
                   jax.ShapeDtypeStruct((share, key_cols), bf16),
                   jax.ShapeDtypeStruct((share, key_cols), bf16)],
        scratch_shapes=[
            V((heads, Z, X, Y, C) + pair, bf16),
            V((heads, flat, HD), bf16), V((heads, flat, HD), bf16),
            V((heads, 2 * rows, HD), bf16), V((heads, 2 * rows, HD), bf16),
            V((flat, 2 * HD), bf16), V((seq, 2 * HD), bf16), V((seq, HD), bf16),
            V((65, rows, HD), f32), V((65, rows, HD), f32),
            V((8, flat), f32), V((8, flat), f32), V((8, flat), f32),
            V((HD, flat), f32), V((2, flat, HD), bf16), V((2, 2 * rows, HD), bf16),
            V((Z * X, Y, C, share, HD), f32), V((Z * X, Y, C, share, HD), f32),
            V((Z, X, Y) + pair, f32), V((2, Y) + pair, f32), V((Y,) + pair, f32),
            V((Z, X, Y) + pair, bf16), V((2, Z, X, Y) + pair, bf16),
            V((Z * X - 1, Y) + pair, bf16), V((heads, Z * X - 1, Y) + pair, bf16),
            V((Y - 1,) + pair, bf16), V((heads, Y - 1) + pair, bf16),
            sem((2, heads, groups)), sem((2, groups)), sem((2, 2, heads, 2)), sem((2, heads, 2)),
            sem((2, Y - 1)), sem((2, heads, Z * X - 1)), sem((2, heads)),
            sem((2, heads)), sem((2, heads, Z * X - 1)), sem((2, heads, Y - 1)),
        ],
        compiler_params=pltpu.CompilerParams(
            collective_id=0, has_side_effects=True, vmem_limit_bytes=65400 << 10),
    )(queries[0], out_grad[0], keys, values)
    return dq[None], dk, dv


def solution(mesh):
    wide = P("section", "ctx", "head")
    tall = P(("section", "ctx"), "head")
    return jax.shard_map(shards, mesh=mesh, in_specs=(wide, wide, tall, tall),
                         out_specs=(wide, tall, tall), check_vma=False)
```

time: 110 us -> 94.1 us (0.86); the launches traced: 108 us -> 93.9 us
  Pallas kernels: 104 us -> 89.3 us
    pallas_call x1, Pallas kernels: 104 us -> 89.3 us  [shards(): pl.pallas_call(kernel, in_specs=[any_space, any_space, in_vmem, in_vmem],...]
where the time goes in v2:
time: 94.1 us; the launch traced here: 93.9 us
  Pallas kernels  89.3 us (95%)
  local copies, waits for them, and re-layouts  3.96 us (4%)
    pallas_call x1, Pallas kernels, shards(): pl.pallas_call(kernel, in_specs=[any_space, any_space, in_vmem, in_vmem],...  89.3 us
    unnamed x7, local copies, waits for them, and re-layouts  3.96 us

profile of v2, /device:TPU:16, one launch (start us, length us, event | category | flops | bytes accessed | tf_op | source)
XLA Modules:
  0.0 93.9 jit_solution(11910139924092286643)
XLA Ops:
  0.6 89.3 %shard_map.67 = (bf16[320,2560]{1,0:T(8,128)(2,1)}, bf16[40,512]{1,0:T(8,128)(2,1)}, bf16[40,512]{1,0:T(8,128)(2,1)}) custom-call(bf16[320,2560]{1,0:T(8,128)(2,1)} %bitcast.3, bf16[320,2560]{1,0:T(8,128)(2,1)} %bitcast.4, bf16[40,512]{1,0:T(8,128)(2,1)} %k_in.1, bf16[40,512]{1,0:T(8,128)(2,1)} %v_in.1), custom_call_target="tpu_custom_call" | custom-call | tf_op jit(solution)/shard_map/pallas_call | solution.py:451
  89.9 0.0 copy-start.1
  90.0 0.0 copy-start
  90.0 2.7 %copy.10 = bf16[1,320,2560]{2,1,0:T(8,128)(2,1)} copy(bf16[1,320,2560]{2,1,0:T(8,128)(2,1)} %bitcast.5) | data formatting | bytes 3276800
  92.7 0.0 copy-done.1
  92.7 0.6 copy.11
  93.3 0.0 copy-done
  93.3 0.6 copy.12
Async XLA Ops:
  89.9 2.7 %copy-start.1 = (bf16[40,512]{1,0:T(8,128)(2,1)S(1)}, bf16[40,512]{1,0:T(8,128)(2,1)}, u32[]{:S(2)}) copy-start(bf16[40,512]{1,0:T(8,128)(2,1)} %get-tuple-element.13) | copy-start | bytes 122884
  90.0 3.4 %copy-start = (bf16[40,512]{1,0:T(8,128)(2,1)S(1)}, bf16[40,512]{1,0:T(8,128)(2,1)}, u32[]{:S(2)}) copy-start(bf16[40,512]{1,0:T(8,128)(2,1)} %get-tuple-element.14) | copy-start | bytes 122884

commit v3 on v2

--- a/solution.py
+++ b/solution.py
@@ -22,30 +22,33 @@
     return lax.dot_general(a, b, (((0,), (0,)), ((), ())), preferred_element_type=f32)
 
 
-def in_pairs(count, step):
-    @pl.loop(0, count // 2)
-    def _(i):
-        step(2 * i)
-        step(2 * i + 1)
-
-    @pl.loop(count // 2 * 2, count)
-    def _(i):
-        step(i)
+def in_groups(count, step, sizes):
+    done = 0
+    for size in sizes:
+        @pl.loop(done // size, count // size)
+        def _(i):
+            for n in range(size):
+                step(size * i + n)
+
+        done = count // size * size
 
 
 CTX = Y * C
+ALONG_Y_LAST = (1, 3)
+CUT = 48
 SHIP = ((0, 4, 0), (5, 5, 1), (6, 7, 2))
 
 
 def kernel(q_hbm, do_hbm, k_in, v_in, dq_hbm, dk_out, dv_out,
            kv, qf, dof, fq, fdo, qs, k2, vv, s_ref, d_ref, m_ref, l_ref, c_ref, dqt, dq_st, fdq_st,
-           dk_acc, dv_acc, own_sum, keep_b, keep_y, cs, cr, bs, br, ys, yr,
-           in_sem, dq_sem, ship_sem, back_sem, gy, gb, gc, rc, rb, ry):
+           dk_acc, dv_acc, own_sum, keep_b, keep_y, cs, cr, bs, br, ys, yr, keep_t, ty, tyr, tb, tbr,
+           in_sem, dq_sem, ship_sem, back_sem, gy, gb, gc, rc, rb, ry, ra, rc2):
     rows = q_hbm.shape[0]
     share = k_in.shape[0]
     heads = k_in.shape[1] // HD
     groups = q_hbm.shape[1] // k_in.shape[1]
     flat = rows * groups
+    last = heads - 1
     scale = HD ** -0.5
     section, ctx, half = lax.axis_index("section"), lax.axis_index("ctx"), lax.axis_index("head")
     z, x, y, c = section // X, section % X, ctx // C, ctx % C
@@ -110,25 +113,30 @@
             src_ref=src, dst_ref=dst, send_sem=sems.at[(0,) + index], recv_sem=sems.at[(1,) + index],
             device_id=where, device_id_type=MESH)
 
-    def gather_y(d):
-        part = kv.at[:, z, x, y, c]
-        return copy(part, part, gy, (d - 1,), y_at[d - 1])
+    def gather_y(h, d):
+        part = kv.at[h, :, :, y, c] if h in ALONG_Y_LAST else kv.at[h, z, x, y, c]
+        return copy(part, part, gy, (h, d - 1), y_at[d - 1])
 
     def gather_b(h, i):
-        part = kv.at[h, z, x, :, c]
+        part = kv.at[h, z, x, y, c] if h in ALONG_Y_LAST else kv.at[h, z, x, :, c]
         return copy(part, part, gb, (h, i), block_at[i])
 
     def gather_c(h):
         part = kv.at[h, :, :, :, c]
         return copy(part, part, gc, (h,), c_at)
 
-    def start_blocks(h):
-        for i in range(len(others)):
-            gather_b(h, i).start()
-
-    def end_blocks(h):
-        for i in range(len(others)):
-            gather_b(h, i).wait_recv()
+    def moves(h, step):
+        if (h in ALONG_Y_LAST) == (step == 0):
+            return [gather_b(h, i) for i in range(len(others))]
+        return [gather_y(h, d) for d in range(1, Y)]
+
+    def start(h, step):
+        for move in moves(h, step):
+            move.start()
+
+    def end(h, step):
+        for move in moves(h, step):
+            move.wait_recv()
 
     def ship(heads_now):
         for is_owner, count in owners:
@@ -140,17 +148,21 @@
                             shipped(h, i, count, 0).start()
                             shipped(h, i, count, 1).start()
 
-    for d in range(1, Y):
-        gather_y(d).start()
+    start(0, 0)
+    start(1, 0)
     ship([0])
-    for d in range(1, Y):
-        gather_y(d).wait_recv()
-    start_blocks(0)
-    ship(range(1, heads))
-    end_blocks(0)
+    end(0, 0)
+    start(0, 1)
+    end(1, 0)
+    start(1, 1)
+    start(2, 0)
+    start(3, 0)
+    ship([1])
+    end(0, 1)
     gather_c(0).start()
-    start_blocks(1)
-    start_blocks(2)
+    end(2, 0)
+    start(2, 1)
+    ship(range(2, heads))
 
     def sum_c(h):
         return copy(cs, cr.at[h % 2], rc, (h,), c_at)
@@ -209,9 +221,73 @@
         for d in range(1, Y):
             sum_y(h, d).wait_recv()
             total = total + yr[h, d - 1].astype(f32)
+        write_out(h, total)
+
+    def write_out(h, total):
         cols = pl.ds(pl.multiple_of(h * HD, HD), HD)
         dk_out[:, cols] = (total[:share] * scale).astype(bf16)
         dv_out[:, cols] = total[share:].astype(bf16)
+
+    def head_rows(ref):
+        return ref.at[:, pl.ds(0, CUT), :]
+
+    def tail_b(i):
+        return copy(head_rows(bs.at[i]), head_rows(br.at[last, i]), rb, (last, i), block_at[i])
+
+    def tail_y(d):
+        return copy(ys.at[d - 1, pl.ds(0, CUT), :], yr.at[last, d - 1, pl.ds(0, CUT), :], ry,
+                    (last, d - 1), y_at[d - 1])
+
+    def tail_y_first(d):
+        return copy(ty.at[d - 1], tyr.at[d - 1], ra, (d - 1,), y_at[d - 1])
+
+    def tail_b_last(i):
+        return copy(tb.at[i], tbr.at[i], rc2, (i,), block_at[i])
+
+    def tail_first():
+        for i in range(len(others)):
+            sum_b(last - 1, i).wait_send()
+        sum_c(last).wait_recv()
+        slot = last % 2
+        for d in range(1, Y):
+            at = (y + d) % Y
+            ty[d - 1] = (own_sum[:, :, at, CUT:] + cr[slot, :, :, at, CUT:].astype(f32)).astype(bf16)
+            tail_y_first(d).start()
+        for i, (bz, bx) in enumerate(block_of):
+            bs[i, :, :CUT] = (own_sum[bz, bx, :, :CUT] + cr[slot, bz, bx, :, :CUT].astype(f32)).astype(bf16)
+            tail_b(i).start()
+        keep_b[slot, :, :CUT] = own_sum[z, x, :, :CUT] + cr[slot, z, x, :, :CUT].astype(f32)
+        keep_t[...] = own_sum[:, :, y, CUT:] + cr[slot, :, :, y, CUT:].astype(f32)
+
+    def tail_second():
+        total = keep_t[...]
+        for d in range(1, Y):
+            tail_y_first(d).wait_recv()
+            total = total + tyr[d - 1].astype(f32)
+        keep_t[...] = total
+        for i, (bz, bx) in enumerate(block_of):
+            tb[i] = keep_t[bz, bx].astype(bf16)
+            tail_b_last(i).start()
+        total = keep_b[last % 2, :, :CUT]
+        for i in range(len(others)):
+            tail_b(i).wait_recv()
+            total = total + br[last, i, :, :CUT].astype(f32)
+        keep_y[:, :CUT] = total
+        for d in range(1, Y):
+            sum_y(last - 1, d).wait_send()
+            ys[d - 1, :CUT] = keep_y[(y + d) % Y, :CUT].astype(bf16)
+            tail_y(d).start()
+
+    def tail_third():
+        below = keep_t[z, x]
+        for i in range(len(others)):
+            tail_b_last(i).wait_recv()
+            below = below + tbr[i].astype(f32)
+        above = keep_y[y, :CUT]
+        for d in range(1, Y):
+            tail_y(d).wait_recv()
+            above = above + yr[last, d - 1, :CUT].astype(f32)
+        write_out(last, jnp.concatenate([above, below], axis=0))
 
     def write_dq(h, g):
         cols = pl.ds(pl.multiple_of((h * groups + g) * HD, HD), HD)
@@ -220,6 +296,9 @@
 
     def lanes_of(width):
         return [(j, min(HD, width - j)) for j in range(0, width, HD)]
+
+    def sizes_of(width):
+        return (4, 2, 1) if width <= 3 * rows else (2, 1)
 
     def begin(width, place, q_part, do_part):
         lanes = lanes_of(width)
@@ -255,7 +334,7 @@
                 c_ref[:, some] = c_ref[:, some] * fade + (e * d).sum(0)
                 m_ref[:, some] = new
 
-        in_pairs(place, lambda b: front(b, False))
+        in_groups(place, lambda b: front(b, False), sizes_of(width))
         front(place, True)
         top8 = m_ref[:, :width]
         top = top8.max(0, keepdims=True)
@@ -289,7 +368,7 @@
                 dk_acc[b] += dk
             dqt[:, :width] += dot_tn(k2[at, :HD], ds)
 
-        in_pairs(place + 1, back)
+        in_groups(place + 1, back, sizes_of(width))
 
     def head(h, carry):
         gather_c(h).wait_recv()
@@ -368,10 +447,11 @@
         for following in range(1, heads):
             @pl.when(h == following - 1)
             def _():
-                end_blocks(following)
+                end(following, 1)
                 gather_c(following).start()
                 if following == 1:
-                    start_blocks(3)
+                    end(3, 0)
+                    start(3, 1)
 
         @pl.when(h >= 1)
         def _():
@@ -400,23 +480,23 @@
 
     lax.fori_loop(0, heads, head, 0)
 
-    last = heads - 1
-    sum_second(last)
+    tail_first()
     sum_last(last - 2)
     sum_third(last - 1)
     sum_last(last - 1)
-    sum_third(last)
-    sum_last(last)
+    tail_second()
+    tail_third()
     for d in range(1, Y):
-        gather_y(d).wait_send()
-        sum_y(last, d).wait_send()
+        tail_y(d).wait_send()
+        tail_y_first(d).wait_send()
+    for i in range(len(others)):
+        tail_b(i).wait_send()
+        tail_b_last(i).wait_send()
     for h in range(heads):
         gather_c(h).wait_send()
-        for i in range(len(others)):
-            gather_b(h, i).wait_send()
+        for move in moves(h, 0) + moves(h, 1):
+            move.wait_send()
     sum_c(last).wait_send()
-    for i in range(len(others)):
-        sum_b(last, i).wait_send()
     for is_owner, count in owners:
         @pl.when(is_owner)
         def _():
@@ -468,9 +548,13 @@
             V((Z, X, Y) + pair, bf16), V((2, Z, X, Y) + pair, bf16),
             V((Z * X - 1, Y) + pair, bf16), V((heads, Z * X - 1, Y) + pair, bf16),
             V((Y - 1,) + pair, bf16), V((heads, Y - 1) + pair, bf16),
+            V((Z, X, 2 * share - CUT, HD), f32),
+            V((Y - 1, Z, X, 2 * share - CUT, HD), bf16), V((Y - 1, Z, X, 2 * share - CUT, HD), bf16),
+            V((Z * X - 1, 2 * share - CUT, HD), bf16), V((Z * X - 1, 2 * share - CUT, HD), bf16),
             sem((2, heads, groups)), sem((2, groups)), sem((2, 2, heads, 2)), sem((2, heads, 2)),
-            sem((2, Y - 1)), sem((2, heads, Z * X - 1)), sem((2, heads)),
+            sem((2, heads, Y - 1)), sem((2, heads, Z * X - 1)), sem((2, heads)),
             sem((2, heads)), sem((2, heads, Z * X - 1)), sem((2, heads, Y - 1)),
+            sem((2, Y - 1)), sem((2, Z * X - 1)),
         ],
         compiler_params=pltpu.CompilerParams(
             collective_id=0, has_side_effects=True, vmem_limit_bytes=65400 << 10),

time: 94.1 us -> 91.4 us (0.971)
  Pallas kernels: 89.3 us -> 86.6 us
    pallas_call x1, Pallas kernels: 89.3 us -> 86.6 us  [shards(): pl.pallas_call(kernel, in_specs=[any_space, any_space, in_vmem, in_vmem],...]
where the time goes in v3:
time: 91.4 us; the launch traced here: 91.2 us
  Pallas kernels  86.6 us (95%)
  local copies, waits for them, and re-layouts  3.96 us (4%)
    pallas_call x1, Pallas kernels, shards(): pl.pallas_call(kernel, in_specs=[any_space, any_space, in_vmem, in_vmem],...  86.6 us
    unnamed x7, local copies, waits for them, and re-layouts  3.96 us

profile of v3, /device:TPU:16, one launch (start us, length us, event | category | flops | bytes accessed | tf_op | source)
XLA Modules:
  0.0 91.2 jit_solution(1190495936523058787)
XLA Ops:
  0.6 86.6 %shard_map.67 = (bf16[320,2560]{1,0:T(8,128)(2,1)}, bf16[40,512]{1,0:T(8,128)(2,1)}, bf16[40,512]{1,0:T(8,128)(2,1)}) custom-call(bf16[320,2560]{1,0:T(8,128)(2,1)} %bitcast.3, bf16[320,2560]{1,0:T(8,128)(2,1)} %bitcast.4, bf16[40,512]{1,0:T(8,128)(2,1)} %k_in.1, bf16[40,512]{1,0:T(8,128)(2,1)} %v_in.1), custom_call_target="tpu_custom_call" | custom-call | tf_op jit(solution)/shard_map/pallas_call | solution.py:531
  87.3 0.0 copy-start.1
  87.3 0.0 copy-start
  87.3 2.7 %copy.10 = bf16[1,320,2560]{2,1,0:T(8,128)(2,1)} copy(bf16[1,320,2560]{2,1,0:T(8,128)(2,1)} %bitcast.5) | data formatting | bytes 3276800
  90.0 0.0 copy-done.1
  90.0 0.6 copy.11
  90.6 0.0 copy-done
  90.6 0.6 copy.12
Async XLA Ops:
  87.3 2.7 %copy-start.1 = (bf16[40,512]{1,0:T(8,128)(2,1)S(1)}, bf16[40,512]{1,0:T(8,128)(2,1)}, u32[]{:S(2)}) copy-start(bf16[40,512]{1,0:T(8,128)(2,1)} %get-tuple-element.13) | copy-start | bytes 122884
  87.3 3.4 %copy-start = (bf16[40,512]{1,0:T(8,128)(2,1)S(1)}, bf16[40,512]{1,0:T(8,128)(2,1)}, u32[]{:S(2)}) copy-start(bf16[40,512]{1,0:T(8,128)(2,1)} %get-tuple-element.14) | copy-start | bytes 122884

commit v4 on v3

--- a/solution.py
+++ b/solution.py
@@ -90,18 +90,17 @@
     helpers = [(low <= CTX - 1 - ctx, CTX - 1 - ctx <= high, count) for low, high, count in SHIP]
     helpers = [(jnp.logical_and(over, under), count) for over, under, count in helpers if count]
 
-    for is_owner, count in owners:
-        @pl.when(is_owner)
-        def _():
-            for h in range(heads):
-                for g in range(groups - count):
-                    load(h, g, 0).start()
-                    load(h, g, 1).start()
-
     barrier = pltpu.get_barrier_semaphore()
     partners = y_at + block_at + [c_at, mirror]
     for partner in partners:
         pl.semaphore_signal(barrier, inc=1, device_id=partner, device_id_type=MESH)
+    for is_owner, count in owners:
+        @pl.when(is_owner)
+        def _():
+            for g in range(groups - count):
+                load(0, g, 0).start()
+                load(0, g, 1).start()
+
     for h in range(heads):
         cols = slice(h * HD, (h + 1) * HD)
         pair = jnp.concatenate([k_in[:, cols].astype(f32), v_in[:, cols].astype(f32)], axis=0)
@@ -153,6 +152,14 @@
     ship([0])
     end(0, 0)
     start(0, 1)
+    for is_owner, count in owners:
+        @pl.when(is_owner)
+        def _():
+            for h in range(1, heads):
+                for g in range(groups - count):
+                    load(h, g, 0).start()
+                    load(h, g, 1).start()
+
     end(1, 0)
     start(1, 1)
     start(2, 0)
@@ -403,7 +410,7 @@
                 for g in range(groups - count):
                     write_dq(h - 2, g).wait()
 
-            dq_st[h % 2, :width] = (dqt[:, :width] * scale).T.astype(bf16)
+            dq_st[h % 2, :width] = (dqt[:, :width] * (scale / 2)).T.astype(bf16)
             for g in range(groups - count):
                 write_dq(h, g).start()
 
@@ -427,7 +434,7 @@
                 for i in range(count):
                     returned(h - 2, i, count).wait_send()
 
-            fdq_st[h % 2, :width] = (dqt[:, :width] * scale).T.astype(bf16)
+            fdq_st[h % 2, :width] = (dqt[:, :width] * (scale / 2)).T.astype(bf16)
             for i in range(count):
                 returned(h, i, count).start()
 
@@ -559,7 +566,7 @@
         compiler_params=pltpu.CompilerParams(
             collective_id=0, has_side_effects=True, vmem_limit_bytes=65400 << 10),
     )(queries[0], out_grad[0], keys, values)
-    return dq[None], dk, dv
+    return (dq * 2)[None], dk, dv
 
 
 def solution(mesh):

time: 91.4 us -> 91.3 us (level)
  other arithmetic: 0 us -> 2.72 us
  local copies, waits for them, and re-layouts: 3.96 us -> 1.24 us
    broadcast_in_dim x0 -> x1, other arithmetic: none -> 2.72 us  [shards(): return ((dq * 2)[None], dk, dv)]
    unnamed x7 -> x6, local copies, waits for them, and re-layouts: 3.96 us -> 1.24 us
where the time goes in v4:
time: 91.3 us; the launch traced here: 91.1 us
  Pallas kernels  86.5 us (95%)
  other arithmetic  2.72 us (3%)
  local copies, waits for them, and re-layouts  1.24 us (1%)
    pallas_call x1, Pallas kernels, shards(): pl.pallas_call(kernel, in_specs=[any_space, any_space, in_vmem, in_vmem],...  86.5 us
    broadcast_in_dim x1, other arithmetic, shards(): return ((dq * 2)[None], dk, dv)  2.72 us

profile of v4, /device:TPU:16, one launch (start us, length us, event | category | flops | bytes accessed | tf_op | source)
XLA Modules:
  0.0 91.1 jit_solution(3345764320540815338)
XLA Ops:
  0.6 86.5 %shard_map.67 = (bf16[320,2560]{1,0:T(8,128)(2,1)}, bf16[40,512]{1,0:T(8,128)(2,1)}, bf16[40,512]{1,0:T(8,128)(2,1)}) custom-call(bf16[320,2560]{1,0:T(8,128)(2,1)} %bitcast.4, bf16[320,2560]{1,0:T(8,128)(2,1)} %bitcast.5, bf16[40,512]{1,0:T(8,128)(2,1)} %k_in.1, bf16[40,512]{1,0:T(8,128)(2,1)} %v_in.1), custom_call_target="tpu_custom_call" | custom-call | tf_op jit(solution)/shard_map/pallas_call | solution.py:538
  87.2 0.0 copy-start.1
  87.2 0.0 copy-start
  87.2 2.7 %multiply_bitcast_fusion = bf16[1,320,2560]{2,1,0:T(8,128)(2,1)} fusion(bf16[320,2560]{1,0:T(8,128)(2,1)} %get-tuple-element.6), kind=kLoop, calls=%fused_computation | loop fusion | flops 819200 | bytes 3276800 | tf_op jit(solution)/shard_map/broadcast_in_dim | solution.py:569
  89.9 0.0 copy-done.1
  89.9 0.6 copy.9
  90.5 0.0 copy-done
  90.5 0.6 copy.10
Async XLA Ops:
  87.2 2.7 %copy-start.1 = (bf16[40,512]{1,0:T(8,128)(2,1)S(1)}, bf16[40,512]{1,0:T(8,128)(2,1)}, u32[]{:S(2)}) copy-start(bf16[40,512]{1,0:T(8,128)(2,1)} %get-tuple-element.13) | copy-start | bytes 122884
  87.2 3.4 %copy-start = (bf16[40,512]{1,0:T(8,128)(2,1)S(1)}, bf16[40,512]{1,0:T(8,128)(2,1)}, u32[]{:S(2)}) copy-start(bf16[40,512]{1,0:T(8,128)(2,1)} %get-tuple-element.14) | copy-start | bytes 122884
